TPU v7x, 32 devices: a whole 2x2x4 slice. The times are simulated.
32 devices in a mesh: dp: 2 (over core), pipe: 2 (over x), ctx: 8 (over z, y).
Axes of the slice: x: 2, y: 2, z: 4, core: 2. Of those that a mesh axis runs over, the one named last changes fastest.
Arguments:
- queries: bfloat16 [4, 1024, 2048], P(('dp', 'pipe'), 'ctx'), parts along dimension 0, may hold values from -6 to 6
- section_key_state: bfloat16 [4, 1024, 256], P(('dp', 'pipe'), 'ctx'), parts along dimension 0, may hold values from -6 to 6
- section_value_state: bfloat16 [4, 1024, 256], P(('dp', 'pipe'), 'ctx'), parts along dimension 0, may hold values from -6 to 6
- out_grad: bfloat16 [4, 1024, 2048], P(('dp', 'pipe'), 'ctx'), parts along dimension 0, may hold values from -6 to 6
- doc_blocks: int32 [4, 4], P(('dp', 'pipe')), parts along dimension 0, may hold values from 1 to 4, 8 in all within a row
Outputs:
- attention: bfloat16 [4, 1024, 2048], P(('dp', 'pipe'), 'ctx'), parts along dimension 0
- query_grads: bfloat16 [4, 1024, 2048], P(('dp', 'pipe'), 'ctx'), parts along dimension 0
- key_grads: bfloat16 [4, 1024, 256], P(('dp', 'pipe'), 'ctx'), parts along dimension 0
- value_grads: bfloat16 [4, 1024, 256], P(('dp', 'pipe'), 'ctx'), parts along dimension 0
There are 2 independent parts, one for each index of `dp`. A program takes and returns all parts, laid end to end along the dimension named above; each array names one. Nothing has to cross between parts.
Inputs may be any that keep to these rules, and one draw needn't show every extreme that they name: `doc_blocks`: each row sums to 8, and one document of each row has exactly 4 blocks.
All inputs are finite; a program needn't handle non-finite values.
Results may differ from a plain program's by a relative error of at most 0.012.
The roundings to bfloat16 on the way count: a program that leaves them out, or rounds other values in their place, can miss the bound.
Values may be sent and summed in bfloat16 or wider, within the bound.
A program may use at most 64 MiB of HBM per device.

v0:
```python
import math

import jax
import jax.numpy as jnp
from jax import lax
from jax.sharding import PartitionSpec as P

QUERY_HEAD_COUNT = 16
KEY_VALUE_HEADS = 2
HEAD_SIZE = 128
BLK = 128


def from_behind(x, axis, by):
    length = lax.axis_size(axis)
    pairs = [(i, i + by) for i in range(length) if 0 <= i + by < length]
    return lax.ppermute(x, axis, pairs)


def layout_positions(device_at, shard_rows, shard_count):
    half_rows = shard_rows // 2
    offsets = jnp.arange(half_rows, dtype=jnp.int32)
    lower_half = device_at * half_rows + offsets
    upper_half = (2 * shard_count - 1 - device_at) * half_rows + offsets
    return jnp.concatenate([lower_half, upper_half], axis=-1).reshape(-1)


def document_of(positions, doc_lengths):
    bounds = (jnp.cumsum(doc_lengths) * BLK)[:-1]
    return jnp.sum((positions[:, None] >= bounds[None, :]).astype(jnp.int32), axis=1)


def to_groups(score_matrix, shard_rows, group_width):
    grouped_heads = score_matrix.reshape(
        shard_rows, KEY_VALUE_HEADS, group_width, HEAD_SIZE
    ).transpose(1, 2, 0, 3)
    return grouped_heads.reshape(KEY_VALUE_HEADS, group_width * shard_rows, HEAD_SIZE)


def from_groups(stacked_values, shard_rows, group_width):
    spread_rows = stacked_values.reshape(
        KEY_VALUE_HEADS, group_width, shard_rows, HEAD_SIZE
    ).transpose(2, 0, 1, 3)
    return spread_rows.reshape(shard_rows, QUERY_HEAD_COUNT * HEAD_SIZE)


def local(queries, section_key_state, section_value_state, out_grad, doc_blocks):
    shard_count = lax.axis_size("ctx")
    shard_rows = queries.shape[1]
    sequence = shard_rows * shard_count
    group_width = QUERY_HEAD_COUNT // KEY_VALUE_HEADS
    piled_rows = group_width * shard_rows
    inverse_root = 1.0 / math.sqrt(HEAD_SIZE)
    block_size = min(512, sequence)
    block_count = sequence // block_size
    term_columns = 2 * KEY_VALUE_HEADS * HEAD_SIZE
    doc_lengths = doc_blocks[0]
    query_pos = layout_positions(lax.axis_index("ctx"), shard_rows, shard_count)
    key_pos = layout_positions(
        jnp.arange(shard_count, dtype=jnp.int32)[:, None], shard_rows, shard_count
    )
    query_doc = document_of(query_pos, doc_lengths)
    key_doc = document_of(key_pos, doc_lengths)
    query_groups = to_groups(queries[0], shard_rows, group_width)
    grad_groups = to_groups(out_grad[0], shard_rows, group_width)
    key_all, value_all = (
        lax.all_gather(section_key_state[0], "ctx", axis=0, tiled=True),
        lax.all_gather(section_value_state[0], "ctx", axis=0, tiled=True),
    )

    def block_inputs(first_row, total_size):
        block_pos = lax.dynamic_slice_in_dim(key_pos, first_row, total_size)
        block_doc = lax.dynamic_slice_in_dim(key_doc, first_row, total_size)
        visible = (query_doc[:, None] == block_doc[None, :]) & (
            block_pos[None, :] <= query_pos[:, None]
        )
        visible = jnp.tile(visible, (group_width, 1))[None]
        key_block = (
            lax.dynamic_slice_in_dim(key_all, first_row, total_size)
            .reshape(total_size, KEY_VALUE_HEADS, HEAD_SIZE)
            .transpose(1, 0, 2)
        )
        value_block = (
            lax.dynamic_slice_in_dim(value_all, first_row, total_size)
            .reshape(total_size, KEY_VALUE_HEADS, HEAD_SIZE)
            .transpose(1, 0, 2)
        )
        return (visible, key_block, value_block)

    def scores_of(visible, key_block):
        scores = jnp.einsum(
            "gqd,gsd->gqs", query_groups, key_block, preferred_element_type=jnp.float32
        )
        return jnp.where(visible, scores * inverse_root, -jnp.inf)

    def stat_step(block_at, carried):
        running_max, running_sum = carried
        visible, key_block, value_block = block_inputs(block_at * block_size, block_size)
        scores = scores_of(visible, key_block)
        new_max = jnp.maximum(running_max, jnp.max(scores, axis=-1))
        new_sum = running_sum * jnp.exp(running_max - new_max)
        new_sum = new_sum + jnp.sum(jnp.exp(scores - new_max[..., None]), axis=-1)
        return (new_max, new_sum)

    initial_max = jnp.full((KEY_VALUE_HEADS, piled_rows), -1e30, jnp.float32)
    initial_sum = jnp.zeros((KEY_VALUE_HEADS, piled_rows), jnp.float32)
    final_max, final_sum = lax.fori_loop(0, block_count, stat_step, (initial_max, initial_sum))
    log_total = final_max + jnp.log(final_sum)

    def out_step(block_at, accumulated):
        visible, key_block, value_block = block_inputs(block_at * block_size, block_size)
        weights_low = jnp.exp(scores_of(visible, key_block) - log_total[..., None]).astype(
            jnp.bfloat16
        )
        return accumulated + jnp.einsum(
            "gqs,gsd->gqd", weights_low, value_block, preferred_element_type=jnp.float32
        )

    blank_output = jnp.zeros((KEY_VALUE_HEADS, piled_rows, HEAD_SIZE), jnp.float32)
    out_groups = lax.fori_loop(0, block_count, out_step, blank_output).astype(jnp.bfloat16)
    row_dot = jnp.sum(grad_groups.astype(jnp.float32) * out_groups.astype(jnp.float32), axis=-1)

    def grads_of(visible, key_block, value_block):
        weights = jnp.exp(scores_of(visible, key_block) - log_total[..., None])
        weight_grad = jnp.einsum(
            "gqd,gsd->gqs", grad_groups, value_block, preferred_element_type=jnp.float32
        )
        score_grad = (weights * (weight_grad - row_dot[..., None]) * inverse_root).astype(
            jnp.bfloat16
        )
        return (weights.astype(jnp.bfloat16), score_grad)

    def key_terms(weights_low, score_grad, total_size):
        key_term = jnp.einsum(
            "gqs,gqd->sgd", score_grad, query_groups, preferred_element_type=jnp.float32
        ).reshape(total_size, KEY_VALUE_HEADS * HEAD_SIZE)
        value_term = jnp.einsum(
            "gqs,gqd->sgd", weights_low, grad_groups, preferred_element_type=jnp.float32
        ).reshape(total_size, KEY_VALUE_HEADS * HEAD_SIZE)
        return jnp.concatenate([key_term, value_term], axis=-1)

    def back_step(query_grad, block_at):
        visible, key_block, value_block = block_inputs(block_at * block_size, block_size)
        weights_low, score_grad = grads_of(visible, key_block, value_block)
        new_grad = query_grad + jnp.einsum(
            "gqs,gsd->gqd", score_grad, key_block, preferred_element_type=jnp.float32
        )
        return (new_grad, key_terms(weights_low, score_grad, block_size))

    blank_gradient = jnp.zeros((KEY_VALUE_HEADS, piled_rows, HEAD_SIZE), jnp.float32)
    query_grad, block_terms = lax.scan(
        back_step, blank_gradient, jnp.arange(block_count, dtype=jnp.int32)
    )
    query_rows = from_groups(query_grad.astype(jnp.bfloat16), shard_rows, group_width)
    pair_sum = lax.psum_scatter(
        block_terms.reshape(sequence, term_columns).astype(jnp.bfloat16),
        "ctx",
        scatter_dimension=0,
        tiled=True,
    )
    joined = jnp.concatenate([query_rows, pair_sum], axis=-1)[None]
    sent_back = from_behind(joined, "pipe", -1)
    query_sent = sent_back[:, :, : QUERY_HEAD_COUNT * HEAD_SIZE]
    pair_passed = sent_back[:, :, QUERY_HEAD_COUNT * HEAD_SIZE :]
    attention = from_groups(out_groups, shard_rows, group_width)[None]
    key_passed = pair_passed[:, :, : KEY_VALUE_HEADS * HEAD_SIZE]
    value_passed = pair_passed[:, :, KEY_VALUE_HEADS * HEAD_SIZE :]
    return (attention, query_sent, key_passed, value_passed)


def solution(mesh):
    return jax.shard_map(
        local,
        mesh=mesh,
        in_specs=(
            P(("dp", "pipe"), "ctx", None),
            P(("dp", "pipe"), "ctx", None),
            P(("dp", "pipe"), "ctx", None),
            P(("dp", "pipe"), "ctx", None),
            P(("dp", "pipe"), None),
        ),
        out_specs=(
            P(("dp", "pipe"), "ctx", None),
            P(("dp", "pipe"), "ctx", None),
            P(("dp", "pipe"), "ctx", None),
            P(("dp", "pipe"), "ctx", None),
        ),
        check_vma=False,
    )
```

profile of v0, /device:TPU:0, one launch (start us, length us, event | category | flops | bytes accessed | tf_op | source)
XLA Modules:
  0.0 227.1 jit_solution(4679452469479922389)
XLA Ops:
  7.3 0.8 reduce-window.9
  8.5 1.1 copy.93
  9.7 0.6 copy.75
  10.3 0.2 reshape.294
  10.5 0.3 copy.78
  10.9 29.5 %all-gather = bf16[1,1024,256]{1,2,0:T(8,128)(2,1)S(1)} all-gather(bf16[1,128,256]{1,2,0:T(8,128)(2,1)S(1)} %copy.74), channel_id=2, replica_groups=mesh['dp'=2,'pipe'=2,'ctx'=8] {'ctx'}, dimensions={1}, use_global_device_ids=true | all-gather | bytes 589824 | tf_op jit(solution)/shard_map/all_gather | solution.py:67
  40.5 14.3 %while.43 = (s32[]{:T(128)}, f32[2,1024]{1,0:T(2,128)S(1)}, f32[2,1024]{1,0:T(2,128)S(1)}, s32[128]{0:T(128)S(1)}, s32[1024]{0:T(1024)S(1)}, /*index=5*/s32[1024...) while((s32[]{:T(128)}, f32[2,1024]{1,0:T(2,128)S(1)}, ...), condition=%wide.region_6.7_spmd.clone, body=%wide.region_3.6_spmd.clone.sunk | while | flops 275982336 | bytes 13096130 | solution.py:107
  40.6 0.2 compare_and_fusion.6
  40.8 0.2 tile.56
  41.1 0.3 copy.113
  41.6 2.8 %fusion.64 = (f32[2,1024]{1,0:T(2,128)S(1)}, f32[2,512,1024]{2,1,0:T(8,128)}) fusion(pred[1024,512]{0,1:T(8,128)(4,1)S(1)} %bitcast.211, bf16[2,1024,128]{2,1,0:T(8,128)(2,1)S(1)} %get-tuple-element.915, bf16[512,2,128]{2,0,1:T(8,128)(2,1)S(1)} %copy.114), kind=kOutput, calls=%fused_computation.2.clone.1 | convolution fusion | flops 271579136 | bytes 5513216 | tf_op jit(solution)/shard_map/while/body/eval_jaxpr/gqd,gsd->gqs/dot_general | solution.py:91
  44.4 3.2 %exponential_reduce_fusion.2 = f32[2,1024]{1,0:T(2,128)S(1)} fusion(f32[2,512,1024]{2,1,0:T(8,128)} %get-tuple-element.852, f32[2,1024]{1,0:T(2,128)S(1)} %fusion.65, pred[1024,512]{0,1:T(8,128)(4,1)S(1)} %bitcast.212), kind=kLoop, calls=%fused_computation.1.clone.1 | loop fusion | flops 4192256 | bytes 4734976 | tf_op jit(solution)/shard_map/while/body/eval_jaxpr/reduce_sum | solution.py:102
  48.0 0.2 tile.56
  48.3 0.3 copy.113
  48.7 2.8 %fusion.64 = (f32[2,1024]{1,0:T(2,128)S(1)}, f32[2,512,1024]{2,1,0:T(8,128)}) fusion(pred[1024,512]{0,1:T(8,128)(4,1)S(1)} %bitcast.211, bf16[2,1024,128]{2,1,0:T(8,128)(2,1)S(1)} %get-tuple-element.915, bf16[512,2,128]{2,0,1:T(8,128)(2,1)S(1)} %copy.114), kind=kOutput, calls=%fused_computation.2.clone.1 | convolution fusion | flops 271579136 | bytes 5513216 | tf_op jit(solution)/shard_map/while/body/eval_jaxpr/gqd,gsd->gqs/dot_general | solution.py:91
  51.6 3.2 %exponential_reduce_fusion.2 = f32[2,1024]{1,0:T(2,128)S(1)} fusion(f32[2,512,1024]{2,1,0:T(8,128)} %get-tuple-element.852, f32[2,1024]{1,0:T(2,128)S(1)} %fusion.65, pred[1024,512]{0,1:T(8,128)(4,1)S(1)} %bitcast.212), kind=kLoop, calls=%fused_computation.1.clone.1 | loop fusion | flops 4192256 | bytes 4734976 | tf_op jit(solution)/shard_map/while/body/eval_jaxpr/reduce_sum | solution.py:102
  54.9 28.8 %all-gather.1 = bf16[1,1024,256]{1,2,0:T(8,128)(2,1)} all-gather(bf16[1,128,256]{1,2,0:T(8,128)(2,1)S(1)} %copy.77), channel_id=3, replica_groups=mesh['dp'=2,'pipe'=2,'ctx'=8] {'ctx'}, dimensions={1}, use_global_device_ids=true | all-gather | bytes 589824 | tf_op jit(solution)/shard_map/all_gather | solution.py:68
  83.8 11.5 %while.44 = (s32[]{:T(128)}, f32[2,1024,128]{2,1,0:T(8,128)}, s32[128]{0:T(128)S(1)}, s32[1024]{0:T(1024)S(1)}, s32[1024]{0:T(1024)S(1)}, /*index=5*/s32[128]{0:...) while((s32[]{:T(128)}, f32[2,1024,128]{2,1,0:T(8,128)}, ...), condition=%wide.region_8.9_spmd.clone, body=%wide.region_7.8_spmd.clone.sunk | while | flops 541786112 | bytes 7492809 | solution.py:120
  84.1 0.2 tile.57
  84.4 0.3 copy.115
  84.6 1.0 constant_dynamic-slice_fusion.9
  86.0 2.9 %fusion.70 = f32[2,1024,128]{2,1,0:T(8,128)} fusion(bf16[2,1024,128]{2,1,0:T(8,128)(2,1)S(1)} %get-tuple-element.955, f32[2,1024]{1,0:T(2,128)S(1)} %get-tuple-element.956, pred[1024,512]{0,1:T(8,128)(4,1)S(1)} %bitcast.225, f32[2,1024,128]{2,1,0:T(8,128)} %get-tuple-element.935, pred[]{:T(512)S(6)} %compare.10, ...), kind=kOutput, calls=%fused_computation.18.clone.1 | convolution fusion | flops 541589504 | bytes 3678209 | tf_op jit(solution)/shard_map/while/body/eval_jaxpr/gqs,gsd->gqd/dot_general | solution.py:115
  89.3 0.2 tile.57
  89.5 0.3 copy.115
  89.8 1.0 constant_dynamic-slice_fusion.9
  91.1 4.1 %fusion.70 = f32[2,1024,128]{2,1,0:T(8,128)} fusion(bf16[2,1024,128]{2,1,0:T(8,128)(2,1)S(1)} %get-tuple-element.955, f32[2,1024]{1,0:T(2,128)S(1)} %get-tuple-element.956, pred[1024,512]{0,1:T(8,128)(4,1)S(1)} %bitcast.225, f32[2,1024,128]{2,1,0:T(8,128)} %get-tuple-element.935, pred[]{:T(512)S(6)} %compare.10, ...), kind=kOutput, calls=%fused_computation.18.clone.1 | convolution fusion | flops 541589504 | bytes 3678209 | tf_op jit(solution)/shard_map/while/body/eval_jaxpr/gqs,gsd->gqd/dot_general | solution.py:115
  95.2 1.4 copy.79
  96.8 0.6 copy.81
  97.4 1.0 reshape.296
  98.4 1.2 multiply_reduce_fusion
  99.7 37.0 %while.45 = (s32[]{:T(128)}, f32[2,1024,128]{2,1,0:T(8,128)}, bf16[2,512,512]{1,2,0:T(8,128)(2,1)}, s32[128]{0:T(128)S(1)}, s32[2]{0:T(128)S(1)}, /*index=5*/s32...) while((s32[]{:T(128)}, f32[2,1024,128]{2,1,0:T(8,128)}, ...), condition=%wide.region_11.12_spmd.clone, body=%wide.region_10.11_spmd.clone.sunk | while | flops 1355481088 | bytes 49190700 | solution.py:151
  99.7 0.6 dynamic_slice.99
  101.3 0.2 tile.58
  101.6 1.1 copy.119
  102.6 1.0 constant_dynamic-slice_fusion.10
  103.8 2.6 %fusion.81 = f32[2,512,1024]{2,1,0:T(8,128)} fusion(bf16[2,1024,128]{1,2,0:T(8,128)(2,1)S(1)} %get-tuple-element.1007, bf16[512,2,128]{2,0,1:T(8,128)(2,1)S(1)} %copy.118), kind=kOutput, calls=%fused_computation.41.clone.1 | convolution fusion | flops 268435456 | bytes 4980736 | tf_op jit(solution)/shard_map/while/body/eval_jaxpr/gqd,gsd->gqs/dot_general | solution.py:91
  106.4 0.9 copy.120
  107.3 4.3 %fusion.82 = bf16[2,1024,512]{1,2,0:T(8,128)(2,1)S(1)} fusion(f32[2,512,1024]{2,1,0:T(8,128)} %fusion.81, bf16[2,1024,128]{1,2,0:T(8,128)(2,1)} %get-tuple-element.1010, f32[2,1024]{1,0:T(2,128)S(1)} %get-tuple-element.1011, f32[2,1024]{1,0:T(2,128)S(1)} %get-tuple-element.1008, pred[1024,512]{0,1:T(8,128)(4,1)} %bitcast.223, ...), kind=kOutput, calls=%fused_computation.28.clone.1 | convolution fusion | flops 275775488 | bytes 7618560 | tf_op jit(solution)/shard_map/while/body/eval_jaxpr/gqd,gsd->gqs/dot_general | solution.py:125
  111.6 0.8 fusion.84
  112.5 2.4 %fusion.83 = bf16[2,512,128]{1,2,0:T(8,128)(2,1)S(1)} fusion(bf16[2,1024,128]{1,2,0:T(8,128)(2,1)} %get-tuple-element.1010, f32[2,512,1024]{2,1,0:T(8,128)S(1)} %copy-done, f32[2,1024]{1,0:T(2,128)S(1)} %get-tuple-element.1008, pred[1024,512]{0,1:T(8,128)(4,1)S(1)} %bitcast.224), kind=kOutput, calls=%fused_computation.33.clone.1 | convolution fusion | flops 272629760 | bytes 5513216 | tf_op jit(solution)/shard_map/while/body/eval_jaxpr/gqs,gqd->sgd/dot_general | solution.py:137
  114.8 0.8 fusion.85
  115.7 1.9 convolution_add_fusion.2
  117.6 0.6 dynamic_slice.99
  119.2 0.2 tile.58
  119.4 1.1 copy.119
  120.5 1.0 constant_dynamic-slice_fusion.10
  121.7 2.6 %fusion.81 = f32[2,512,1024]{2,1,0:T(8,128)} fusion(bf16[2,1024,128]{1,2,0:T(8,128)(2,1)S(1)} %get-tuple-element.1007, bf16[512,2,128]{2,0,1:T(8,128)(2,1)S(1)} %copy.118), kind=kOutput, calls=%fused_computation.41.clone.1 | convolution fusion | flops 268435456 | bytes 4980736 | tf_op jit(solution)/shard_map/while/body/eval_jaxpr/gqd,gsd->gqs/dot_general | solution.py:91
  124.3 0.9 copy.120
  125.2 4.3 %fusion.82 = bf16[2,1024,512]{1,2,0:T(8,128)(2,1)S(1)} fusion(f32[2,512,1024]{2,1,0:T(8,128)} %fusion.81, bf16[2,1024,128]{1,2,0:T(8,128)(2,1)} %get-tuple-element.1010, f32[2,1024]{1,0:T(2,128)S(1)} %get-tuple-element.1011, f32[2,1024]{1,0:T(2,128)S(1)} %get-tuple-element.1008, pred[1024,512]{0,1:T(8,128)(4,1)} %bitcast.223, ...), kind=kOutput, calls=%fused_computation.28.clone.1 | convolution fusion | flops 275775488 | bytes 7618560 | tf_op jit(solution)/shard_map/while/body/eval_jaxpr/gqd,gsd->gqs/dot_general | solution.py:125
  129.5 0.8 fusion.84
  130.3 2.4 %fusion.83 = bf16[2,512,128]{1,2,0:T(8,128)(2,1)S(1)} fusion(bf16[2,1024,128]{1,2,0:T(8,128)(2,1)} %get-tuple-element.1010, f32[2,512,1024]{2,1,0:T(8,128)S(1)} %copy-done, f32[2,1024]{1,0:T(2,128)S(1)} %get-tuple-element.1008, pred[1024,512]{0,1:T(8,128)(4,1)S(1)} %bitcast.224), kind=kOutput, calls=%fused_computation.33.clone.1 | convolution fusion | flops 272629760 | bytes 5513216 | tf_op jit(solution)/shard_map/while/body/eval_jaxpr/gqs,gqd->sgd/dot_general | solution.py:137
  132.7 0.8 fusion.85
  133.5 3.1 %convolution_add_fusion.2 = f32[2,1024,128]{2,1,0:T(8,128)} fusion(bf16[2,1024,512]{1,2,0:T(8,128)(2,1)S(1)} %fusion.82, f32[2,1024,128]{2,1,0:T(8,128)} %get-tuple-element.981, pred[]{:T(512)S(6)} %compare.11, bf16[512,2,128]{2,0,1:T(8,128)(2,1)S(1)} %copy.118), kind=kOutput, calls=%fused_computation.36.clone.1 | convolution fusion | flops 268959744 | bytes 4456449 | tf_op jit(solution)/shard_map/while/body/eval_jaxpr/gqs,gsd->gqd/dot_general | solution.py:145
  136.7 2.3 %copy.83 = bf16[2,512,512]{2,1,0:T(8,128)(2,1)} copy(bf16[2,512,512]{1,2,0:T(8,128)(2,1)} %get-tuple-element.405) | data formatting | bytes 2097152 | tf_op jit(solution)/shard_map/convert_element_type | solution.py:156
  139.1 1.3 convert_element_type.42
  140.4 0.3 copy.82
  140.8 60.1 %reduce-scatter.2.cloned.1.call-done = bf16[128,512]{1,0:T(8,128)(2,1)} async-done(((bf16[1024,512]{1,0:T(8,128)(2,1)}), bf16[128,512]{1,0:T(8,128)(2,1)}) %reduce-scatter.2.cloned.1.call-update) | async-done | bytes 131088 | tf_op jit(solution)/shard_map/reduce_scatter | solution.py:155
  201.0 0.9 maximum_bitcast_fusion.1
  201.9 1.3 collective-permute-start
  203.3 0.6 copy.80
  203.9 1.0 broadcast_in_dim_reshape.4
  205.0 13.8 %collective-permute-done = bf16[1,128,2560]{2,1,0:T(8,128)(2,1)S(1)} collective-permute-done((bf16[1,128,2560]{2,1,0:T(8,128)(2,1)S(1)}, bf16[1,128,2560]{2,1,0:T(8,128)(2,1)S(1)}, u32[]{:S(2)}, u32[]{:S(2)}) %collective-permute-start) | collective-permute-done | bytes 655392 | tf_op jit(solution)/shard_map/ppermute | solution.py:17
  218.8 0.8 slice.24
  219.6 0.7 fusion.30
  (75 shorter events, 4.5 us)
Async XLA Ops:
  7.2 3.6 %copy-start.5 = (bf16[1,128,256]{2,1,0:T(8,128)(2,1)S(1)}, bf16[1,128,256]{2,1,0:T(8,128)(2,1)}, u32[]{:S(2)}) copy-start(bf16[1,128,256]{2,1,0:T(8,128)(2,1)} %param.12) | copy-start | bytes 196612
  7.2 193.8 %reduce-scatter.2.cloned.1.call-start = ((), (), s32[]{:S(2)}) async-start(), calls=%async_computation.1 | async-start | bytes 1179648 | tf_op jit(solution)/shard_map/reduce_scatter | solution.py:155
  40.5 14.3 %copy-start.6 = (bf16[1,128,256]{2,1,0:T(8,128)(2,1)S(1)}, bf16[1,128,256]{2,1,0:T(8,128)(2,1)}, u32[]{:S(2)}) copy-start(bf16[1,128,256]{2,1,0:T(8,128)(2,1)} %param.13) | copy-start | bytes 196612
  83.7 13.0 %copy-start.4 = (bf16[1,128,2048]{2,1,0:T(8,128)(2,1)S(1)}, bf16[1,128,2048]{2,1,0:T(8,128)(2,1)}, u32[]{:S(2)}) copy-start(bf16[1,128,2048]{2,1,0:T(8,128)(2,1)} %param.14) | copy-start | bytes 1572868
  96.7 3.0 %copy-start.2 = (bf16[2,1024,128]{1,2,0:T(8,128)(2,1)}, bf16[2,1024,128]{1,2,0:T(8,128)(2,1)S(1)}, u32[]{:S(2)}) copy-start(bf16[2,1024,128]{1,2,0:T(8,128)(2,1)S(1)} %copy.79) | copy-start | bytes 1572868
  107.3 5.2 %copy-start = (f32[2,512,1024]{2,1,0:T(8,128)S(1)}, f32[2,512,1024]{2,1,0:T(8,128)}, u32[]{:S(2)}) copy-start(f32[2,512,1024]{2,1,0:T(8,128)} %fusion.81) | copy-start | bytes 12582916 | tf_op jit(solution)/shard_map/while
  107.3 5.2 %copy-start.1 = (pred[64,8,8,128]{3,1,2,0:T(8,128)(4,1)S(1)}, pred[64,8,8,128]{3,1,2,0:T(8,128)(4,1)}, u32[]{:S(2)}) copy-start(pred[64,8,8,128]{3,1,2,0:T(8,128)(4,1)} %copy.119) | copy-start | bytes 1572868 | tf_op jit(solution)/shard_map/while
  125.1 5.2 %copy-start = (f32[2,512,1024]{2,1,0:T(8,128)S(1)}, f32[2,512,1024]{2,1,0:T(8,128)}, u32[]{:S(2)}) copy-start(f32[2,512,1024]{2,1,0:T(8,128)} %fusion.81) | copy-start | bytes 12582916 | tf_op jit(solution)/shard_map/while
  125.1 5.2 %copy-start.1 = (pred[64,8,8,128]{3,1,2,0:T(8,128)(4,1)S(1)}, pred[64,8,8,128]{3,1,2,0:T(8,128)(4,1)}, u32[]{:S(2)}) copy-start(pred[64,8,8,128]{3,1,2,0:T(8,128)(4,1)} %copy.119) | copy-start | bytes 1572868 | tf_op jit(solution)/shard_map/while
  136.7 66.6 %copy-start.3 = (bf16[2,1024,128]{1,2,0:T(8,128)(2,1)S(1)}, bf16[2,1024,128]{1,2,0:T(8,128)(2,1)}, u32[]{:S(2)}) copy-start(bf16[2,1024,128]{1,2,0:T(8,128)(2,1)} %copy-done.2) | copy-start | bytes 1572868
  201.9 16.8 %collective-permute-start = (bf16[1,128,2560]{2,1,0:T(8,128)(2,1)S(1)}, bf16[1,128,2560]{2,1,0:T(8,128)(2,1)S(1)}, u32[]{:S(2)}, u32[]{:S(2)}) collective-permute-start(bf16[1,128,2560]{2,1,0:T(8,128)(2,1)S(1)} %maximum_bitcast_fusion.1), channel_id=1, source_target_pairs={{8,0},{9,1},{10,2},{11,3},{12,4},{13,5},{14,6},{15,7},{24,16},{25,... | collective-permute-start | bytes 1966088 | tf_op jit(solution)/shard_map/ppermute | solution.py:17
Sparse Core Ops, SparseCore 0:
  139.2 61.7 reduce-scatter.1
where the time goes:
time: 228 us; the launch traced here: 227 us
  waiting for transfers between devices  74 us (32%)
  blocking collectives  58.3 us (26%)
  matrix products  38 us (17%)
  local copies, waits for them, and re-layouts  25.5 us (11%)
  between operations  14.3 us (6%)
  other arithmetic  14 us (6%)
    reduce_scatter x1, waiting for transfers between devices, local(): lax.psum_scatter(block_terms.reshape(sequence, term_columns).astype(jnp.b...  60.1 us
    all_gather x1, blocking collectives, local(): lax.all_gather(section_key_state[0], 'ctx', axis=0, tiled=True)  29.5 us
    all_gather x1, blocking collectives, local(): lax.all_gather(section_value_state[0], 'ctx', axis=0, tiled=True)  28.8 us
    ppermute x1, waiting for transfers between devices, from_behind(): return lax.ppermute(x, axis, pairs)  13.8 us
    dot_general x4, matrix products, scores_of(): jnp.einsum('gqd,gsd->gqs', query_groups, key_block, preferred_element_typ...  11 us
    dot_general x2, matrix products, grads_of(): jnp.einsum('gqd,gsd->gqs', grad_groups, value_block, preferred_element_ty...  8.62 us
    dot_general x2, matrix products, out_step(): jnp.einsum('gqs,gsd->gqd', weights_low, value_block, preferred_element_ty...  6.99 us
    reduce_sum x2, other arithmetic, stat_step(): new_sum = new_sum + jnp.sum(jnp.exp(scores - new_max[..., None]), axis=-1)  6.32 us
  transfers between devices with their start and end apart: 2, of which 2 were waited for; matrix products, arithmetic and copies ran while one was open for 2% of the time, Pallas kernels for 0%

commit v1 on v0

v1 whole, which is shorter than its diff:
```python
import functools
import math

import jax
import jax.numpy as jnp
from jax import lax
from jax.experimental import pallas as pl
from jax.experimental.pallas import tpu as pltpu
from jax.sharding import PartitionSpec as P

KEY_VALUE_HEADS = 2
HEAD_SIZE = 128
BLK = 128
LOG2E = math.log2(math.e)
F32 = jnp.float32
BF16 = jnp.bfloat16


def dot(a, b, contract):
    return lax.dot_general(a, b, (contract, ((), ())), preferred_element_type=F32)


def kernel(
    count, sections, heads, docs,
    doc_ref, q_ref, k_ref, v_ref, go_ref,
    att_ref, qg_ref, kg_ref, vg_ref,
    kv, acc, dkv, recv, probs, dq, fin,
    kv_send, kv_recv, part_send, part_recv, dq_send, dq_recv, fin_send, fin_recv,
):
    rows = q_ref.shape[1]
    half = rows // 2
    width = KEY_VALUE_HEADS * HEAD_SIZE
    group = heads // KEY_VALUE_HEADS
    lanes = group * half
    span = count * half
    scale = 1.0 / math.sqrt(HEAD_SIZE)
    me = lax.axis_index("ctx")
    section = lax.axis_index("pipe")
    has_grads = section > 0
    has_next = section < sections - 1

    def block_rows(block):
        return pl.ds(pl.multiple_of(block * half, half), half)

    def start_of(c):
        return 2 * ((2 * count - 1 - c) // 2) - count + 2

    def upper_of(d):
        return 2 * count - 1 - d

    def upper_used(c, d):
        return c <= d

    def lower_for_upper(c, d):
        return d >= start_of(c)

    def lower_used(c, d):
        return (d <= c) | (d >= start_of(c))

    kv[...] = jnp.zeros_like(kv)
    kv[block_rows(me), :width] = k_ref[0, :half, :]
    kv[block_rows(me), width:] = v_ref[0, :half, :]
    kv[block_rows(upper_of(me)), :width] = k_ref[0, half:, :]
    kv[block_rows(upper_of(me)), width:] = v_ref[0, half:, :]

    barrier = pltpu.get_barrier_semaphore()
    MESH = pl.DeviceIdType.MESH
    for step in range(1, count):
        pl.semaphore_signal(
            barrier, inc=1, device_id={"ctx": lax.rem(me + step, count)}, device_id_type=MESH
        )

    @pl.when(has_grads)
    def _():
        pl.semaphore_signal(barrier, inc=1, device_id={"pipe": section - 1}, device_id_type=MESH)

    @pl.when(has_next)
    def _():
        pl.semaphore_signal(barrier, inc=1, device_id={"pipe": section + 1}, device_id_type=MESH)

    pl.semaphore_wait(
        barrier, count - 1 + jnp.minimum(section, 1) + jnp.minimum(sections - 1 - section, 1)
    )

    def kv_copy(block, part, step_send, step_recv, target):
        return pltpu.make_async_remote_copy(
            src_ref=kv.at[block_rows(block)],
            dst_ref=kv.at[block_rows(block)],
            send_sem=kv_send.at[step_send, part],
            recv_sem=kv_recv.at[step_recv, part],
            device_id={"ctx": target},
            device_id_type=MESH,
        )

    for step in range(1, count):
        to = lax.rem(me + step, count)

        @pl.when(upper_used(to, me))
        def _():
            kv_copy(upper_of(me), 1, step, step, to).start()

        @pl.when(lower_used(to, me))
        def _():
            kv_copy(me, 0, step, step, to).start()

    acc[...] = jnp.zeros_like(acc)

    @pl.when(jnp.logical_not(has_next))
    def _():
        qg_ref[...] = jnp.zeros_like(qg_ref)
        kg_ref[...] = jnp.zeros_like(kg_ref)
        vg_ref[...] = jnp.zeros_like(vg_ref)

    def kv_wait(step, part, source, block):
        kv_copy(block, part, step, step, source).wait_recv()

    def stack(ref, part, g):
        return jnp.concatenate(
            [
                ref[0, part * half:(part + 1) * half, h * HEAD_SIZE:(h + 1) * HEAD_SIZE]
                for h in range(g * group, (g + 1) * group)
            ],
            axis=0,
        )

    def unstack(ref, part, g, value):
        for j in range(group):
            h = g * group + j
            ref[0, part * half:(part + 1) * half, h * HEAD_SIZE:(h + 1) * HEAD_SIZE] = value[
                j * half:(j + 1) * half
            ]

    def dq_copy(part, g):
        index = part * KEY_VALUE_HEADS + g
        cut = (
            slice(None),
            pl.ds(part * half, half),
            pl.ds(g * group * HEAD_SIZE, group * HEAD_SIZE),
        )
        return pltpu.make_async_remote_copy(
            src_ref=dq.at[cut],
            dst_ref=qg_ref.at[cut],
            send_sem=dq_send.at[index],
            recv_sem=dq_recv.at[index],
            device_id={"pipe": section - 1},
            device_id_type=MESH,
        )

    def unit(part, g):
        first = start_of(me) if part else 0
        own = upper_of(me) if part else me
        base = first * half
        window = pl.ds(pl.multiple_of(base, BLK), span) if part else pl.ds(0, span)
        key_cols = slice(g * HEAD_SIZE, (g + 1) * HEAD_SIZE)
        value_cols = slice(width + g * HEAD_SIZE, width + (g + 1) * HEAD_SIZE)
        query = stack(q_ref, part, g)
        grad = stack(go_ref, part, g)
        keys = kv[window, key_cols]
        values = kv[window, value_cols]
        bound = jnp.int32(0)
        low = jnp.int32(0)
        for j in range(docs - 1):
            bound = bound + doc_ref[0, j] * BLK
            low = jnp.where(bound <= own * half, bound, low)
        key_pos = base + lax.broadcasted_iota(jnp.int32, (span, lanes), 0)
        query_pos = own * half + lax.broadcasted_iota(jnp.int32, (span, lanes), 1) % half
        visible = (key_pos >= low) & (key_pos <= query_pos)
        scores = dot(keys, query, ((1,), (1,))) * (scale * LOG2E)
        scores = jnp.where(visible, scores, -jnp.inf)
        top = jnp.max(scores, axis=0, keepdims=True)
        weights = jnp.exp2(scores - top)
        weights = weights * (1.0 / jnp.sum(weights, axis=0, keepdims=True))
        probs[...] = weights
        low_weights = weights.astype(BF16)
        out = dot(values.T, low_weights, ((1,), (0,))).astype(BF16)
        unstack(att_ref, part, g, out.T)

        @pl.when(has_grads)
        def _():
            delta = jnp.sum(grad.T.astype(F32) * out.astype(F32), axis=0, keepdims=True)
            weight_grad = dot(values, grad, ((1,), (1,)))
            p = probs[...]
            score_grad = (p * (weight_grad - delta) * scale).astype(BF16)
            query_grad = dot(keys.T, score_grad, ((1,), (0,))).astype(BF16)
            unstack(dq, part, g, query_grad.T)
            dq_copy(part, g).start()
            acc[window, key_cols] += dot(score_grad, query, ((1,), (0,)))
            acc[window, value_cols] += dot(p.astype(BF16), grad, ((1,), (0,)))

    def part_copy(block, part, owner, step):
        return pltpu.make_async_remote_copy(
            src_ref=dkv.at[block_rows(block)],
            dst_ref=recv.at[step, part],
            send_sem=part_send.at[step, part],
            recv_sem=part_recv.at[step, part],
            device_id={"ctx": owner},
            device_id_type=MESH,
        )

    for step in range(1, count):
        source = lax.rem(me + count - step, count)

        @pl.when(upper_used(me, source))
        def _():
            kv_wait(step, 1, source, upper_of(source))

        @pl.when(lower_for_upper(me, source))
        def _():
            kv_wait(step, 0, source, source)

    for g in range(KEY_VALUE_HEADS):
        unit(1, g)

    @pl.when(has_grads)
    def _():
        dkv[span:, :] = acc[span:, :].astype(BF16)
        for step in range(1, count):
            owner = lax.rem(me + step, count)

            @pl.when(upper_used(me, owner))
            def _():
                part_copy(upper_of(owner), 1, owner, step).start()

    for step in range(1, count):
        source = lax.rem(me + count - step, count)

        @pl.when(lower_used(me, source) & jnp.logical_not(lower_for_upper(me, source)))
        def _():
            kv_wait(step, 0, source, source)

    for g in range(KEY_VALUE_HEADS):
        unit(0, g)

    @pl.when(has_grads)
    def _():
        dkv[:span, :] = acc[:span, :].astype(BF16)
        for step in range(1, count):
            owner = lax.rem(me + step, count)

            @pl.when(lower_used(me, owner))
            def _():
                part_copy(owner, 0, owner, step).start()

        def fin_copy(index):
            out = (kg_ref, vg_ref)[index]
            return pltpu.make_async_remote_copy(
                src_ref=fin.at[pl.ds(index, 1)],
                dst_ref=out,
                send_sem=fin_send.at[index],
                recv_sem=fin_recv.at[index],
                device_id={"pipe": section - 1},
                device_id_type=MESH,
            )

        for part in (1, 0):
            block = upper_of(me) if part else me
            used = upper_used if part else lower_used
            acc[:half, :] = dkv[block_rows(block), :].astype(F32)
            for step in range(1, count):
                source = lax.rem(me + count - step, count)

                @pl.when(used(source, me))
                def _():
                    part_copy(block, part, source, step).wait_recv()
                    acc[:half, :] += recv[step, part].astype(F32)

            total = acc[:half, :].astype(BF16)
            fin[0, part * half:(part + 1) * half, :] = total[:, :width]
            fin[1, part * half:(part + 1) * half, :] = total[:, width:]
        for index in range(2):
            fin_copy(index).start()
        for step in range(1, count):
            owner = lax.rem(me + step, count)

            @pl.when(upper_used(me, owner))
            def _():
                part_copy(upper_of(owner), 1, owner, step).wait_send()

            @pl.when(lower_used(me, owner))
            def _():
                part_copy(owner, 0, owner, step).wait_send()

        for part in (1, 0):
            for g in range(KEY_VALUE_HEADS):
                dq_copy(part, g).wait_send()
        for index in range(2):
            fin_copy(index).wait_send()

    for step in range(1, count):
        to = lax.rem(me + step, count)

        @pl.when(upper_used(to, me))
        def _():
            kv_copy(upper_of(me), 1, step, step, to).wait_send()

        @pl.when(lower_used(to, me))
        def _():
            kv_copy(me, 0, step, step, to).wait_send()

    @pl.when(has_next)
    def _():
        for part in (1, 0):
            for g in range(KEY_VALUE_HEADS):
                dq_copy(part, g).wait_recv()
        for index in range(2):
            pltpu.make_async_remote_copy(
                src_ref=fin.at[pl.ds(index, 1)],
                dst_ref=(kg_ref, vg_ref)[index],
                send_sem=fin_send.at[index],
                recv_sem=fin_recv.at[index],
                device_id={"pipe": section + 1},
                device_id_type=MESH,
            ).wait_recv()


def solution(mesh):
    count, sections = mesh.shape["ctx"], mesh.shape["pipe"]

    def local(queries, keys, values, out_grad, doc_blocks):
        rows, columns = queries.shape[1:]
        half = rows // 2
        width = keys.shape[2]
        span = count * half
        heads = columns // HEAD_SIZE
        group = heads // KEY_VALUE_HEADS
        vmem = pl.BlockSpec(memory_space=pltpu.VMEM)
        dma = pltpu.SemaphoreType.DMA
        shape = jax.ShapeDtypeStruct
        return pl.pallas_call(
            functools.partial(kernel, count, sections, heads, doc_blocks.shape[1]),
            out_shape=(
                shape(queries.shape, BF16),
                shape(queries.shape, BF16),
                shape(keys.shape, BF16),
                shape(values.shape, BF16),
            ),
            in_specs=[pl.BlockSpec(memory_space=pltpu.SMEM)] + [vmem] * 4,
            out_specs=(vmem,) * 4,
            scratch_shapes=[
                pltpu.VMEM((2 * span, 2 * width), BF16),
                pltpu.VMEM((2 * span, 2 * width), F32),
                pltpu.VMEM((2 * span, 2 * width), BF16),
                pltpu.VMEM((count, 2, half, 2 * width), BF16),
                pltpu.VMEM((span, group * half), F32),
                pltpu.VMEM(queries.shape, BF16),
                pltpu.VMEM((2, rows, width), BF16),
                dma((count, 2)),
                dma((count, 2)),
                dma((count, 2)),
                dma((count, 2)),
                dma((2 * KEY_VALUE_HEADS,)),
                dma((2 * KEY_VALUE_HEADS,)),
                dma((2,)),
                dma((2,)),
            ],
            compiler_params=pltpu.CompilerParams(
                collective_id=0, has_side_effects=True, vmem_limit_bytes=40 << 20
            ),
        )(doc_blocks, queries, keys, values, out_grad)

    split = P(("dp", "pipe"), "ctx", None)
    return jax.shard_map(
        local,
        mesh=mesh,
        in_specs=(split, split, split, split, P(("dp", "pipe"), None)),
        out_specs=(split,) * 4,
        check_vma=False,
    )
```

time: 228 us -> 51.9 us (0.23)
  the two profiles are of different devices: /device:TPU:0 before, /device:TPU:28 now
where the time goes in v1:
time: 51.9 us; the launch traced here: 51.6 us
  Pallas kernels  43.7 us (84%)
  local copies, waits for them, and re-layouts  7.25 us (14%)
  between operations  0.65 us (1%)
    pallas_call x1, Pallas kernels, local(): pl.pallas_call(functools.partial(kernel, count, sections, heads, doc_bloc...  43.7 us
    unnamed x14, local copies, waits for them, and re-layouts  7.25 us

profile of v1, /device:TPU:28, one launch (start us, length us, event | category | flops | bytes accessed | tf_op | source)
XLA Modules:
  0.0 51.6 jit_solution(6221616618011199412)
XLA Ops:
  0.6 0.0 copy-start
  0.6 1.0 %copy-done = bf16[1,128,2048]{2,1,0:T(8,128)(2,1)S(1)} copy-done((bf16[1,128,2048]{2,1,0:T(8,128)(2,1)S(1)}, bf16[1,128,2048]{2,1,0:T(8,128)(2,1)}, u32[]{:S(2)}) %copy-start) | copy-done | bytes 524312
  1.7 0.0 copy-start.1
  1.7 1.0 %copy-done.1 = bf16[1,128,2048]{2,1,0:T(8,128)(2,1)S(1)} copy-done((bf16[1,128,2048]{2,1,0:T(8,128)(2,1)S(1)}, bf16[1,128,2048]{2,1,0:T(8,128)(2,1)}, u32[]{:S(2)}) %copy-start.1) | copy-done | bytes 524312
  2.7 0.0 copy-start.2
  2.7 0.8 %copy-done.2 = bf16[1,128,256]{2,1,0:T(8,128)(2,1)S(1)} copy-done((bf16[1,128,256]{2,1,0:T(8,128)(2,1)S(1)}, bf16[1,128,256]{2,1,0:T(8,128)(2,1)}, u32[]{:S(2)}) %copy-start.2) | copy-done | bytes 65560
  3.6 0.0 copy-start.3
  3.6 0.8 %copy-done.3 = bf16[1,128,256]{2,1,0:T(8,128)(2,1)S(1)} copy-done((bf16[1,128,256]{2,1,0:T(8,128)(2,1)S(1)}, bf16[1,128,256]{2,1,0:T(8,128)(2,1)}, u32[]{:S(2)}) %copy-start.3) | copy-done | bytes 65560
  4.4 0.0 copy-start.4
  4.4 0.7 %copy-done.4 = s32[1,4]{1,0:T(1,128)S(1)} copy-done((s32[1,4]{1,0:T(1,128)S(1)}, s32[1,4]{1,0:T(1,128)}, u32[]{:S(2)}) %copy-start.4) | copy-done | bytes 40
  5.1 43.7 %shard_map.84 = (bf16[1,128,2048]{2,1,0:T(8,128)(2,1)S(1)}, bf16[1,128,2048]{2,1,0:T(8,128)(2,1)S(1)}, bf16[1,128,256]{2,1,0:T(8,128)(2,1)S(1)}, bf16[1,128,256]{2,1,0:T(8,128)(2,1)S(1)}) custom-call(s32[1,4]{1,0:T(1,128)S(1)} %copy-done.4, bf16[1,128,2048]{2,1,0:T(8,128)(2,1)S(1)} %copy-done, bf16[1,128,256]{2,1,0:T(8,128)(2,1)S(1)} %copy-done.2, ...), custom_call_target="tpu_custom_call" | custom-call | tf_op jit(solution)/shard_map/pallas_call | solution.py:329
  48.7 0.8 %copy.13 = bf16[1,128,2048]{2,1,0:T(8,128)(2,1)} copy(bf16[1,128,2048]{2,1,0:T(8,128)(2,1)S(1)} %get-tuple-element.8) | data formatting | bytes 1048576
  49.5 0.8 %copy.14 = bf16[1,128,2048]{2,1,0:T(8,128)(2,1)} copy(bf16[1,128,2048]{2,1,0:T(8,128)(2,1)S(1)} %get-tuple-element.9) | data formatting | bytes 1048576
  50.3 0.6 %copy.15 = bf16[1,128,256]{2,1,0:T(8,128)(2,1)} copy(bf16[1,128,256]{2,1,0:T(8,128)(2,1)S(1)} %get-tuple-element.10) | data formatting | bytes 131072
  50.9 0.6 %copy.16 = bf16[1,128,256]{2,1,0:T(8,128)(2,1)} copy(bf16[1,128,256]{2,1,0:T(8,128)(2,1)S(1)} %get-tuple-element.11) | data formatting | bytes 131072
Async XLA Ops:
  0.6 1.0 %copy-start = (bf16[1,128,2048]{2,1,0:T(8,128)(2,1)S(1)}, bf16[1,128,2048]{2,1,0:T(8,128)(2,1)}, u32[]{:S(2)}) copy-start(bf16[1,128,2048]{2,1,0:T(8,128)(2,1)} %q_ref.1) | copy-start | bytes 1572868
  1.7 1.0 %copy-start.1 = (bf16[1,128,2048]{2,1,0:T(8,128)(2,1)S(1)}, bf16[1,128,2048]{2,1,0:T(8,128)(2,1)}, u32[]{:S(2)}) copy-start(bf16[1,128,2048]{2,1,0:T(8,128)(2,1)} %go_ref.1) | copy-start | bytes 1572868
  2.7 0.8 %copy-start.2 = (bf16[1,128,256]{2,1,0:T(8,128)(2,1)S(1)}, bf16[1,128,256]{2,1,0:T(8,128)(2,1)}, u32[]{:S(2)}) copy-start(bf16[1,128,256]{2,1,0:T(8,128)(2,1)} %k_ref.1) | copy-start | bytes 196612
  3.6 0.8 %copy-start.3 = (bf16[1,128,256]{2,1,0:T(8,128)(2,1)S(1)}, bf16[1,128,256]{2,1,0:T(8,128)(2,1)}, u32[]{:S(2)}) copy-start(bf16[1,128,256]{2,1,0:T(8,128)(2,1)} %v_ref.1) | copy-start | bytes 196612
  4.4 0.7 %copy-start.4 = (s32[1,4]{1,0:T(1,128)S(1)}, s32[1,4]{1,0:T(1,128)}, u32[]{:S(2)}) copy-start(s32[1,4]{1,0:T(1,128)} %doc_ref.1) | copy-start | bytes 52

commit v2 on v1

v2 whole, which is shorter than its diff:
```python
import functools
import math

import jax
import jax.numpy as jnp
from jax import lax
from jax.experimental import pallas as pl
from jax.experimental.pallas import tpu as pltpu
from jax.sharding import PartitionSpec as P

KEY_VALUE_HEADS = 2
HEAD_SIZE = 128
BLK = 128
LOG2E = math.log2(math.e)
F32 = jnp.float32
BF16 = jnp.bfloat16


def dot(a, b, contract):
    return lax.dot_general(a, b, (contract, ((), ())), preferred_element_type=F32)


def kernel(
    count, sections, heads, docs,
    doc_in, q_in, k_in, v_in, go_in,
    att_ref, qg_ref, kg_ref, vg_ref,
    doc_ref, q_ref, go_ref, k_ref, v_ref,
    kv, acc, dkv, pair, paired, recv, probs, dq, fin,
    load_sem, line_send, line_recv, side_send, side_recv,
    pair_send, pair_recv, sum_send, sum_recv,
    dq_send, dq_recv, fin_send, fin_recv,
):
    rows = q_ref.shape[1]
    half = rows // 2
    group = heads // KEY_VALUE_HEADS
    lanes = group * half
    span = count * half
    pairs = count // 2
    scale = 1.0 / math.sqrt(HEAD_SIZE)
    me = lax.axis_index("ctx")
    line = me // 2
    side = me % 2
    partner = line * 2 + 1 - side
    section = lax.axis_index("pipe")
    has_grads = section > 0
    has_next = section < sections - 1
    MESH = pl.DeviceIdType.MESH

    loads = [
        pltpu.make_async_copy(source, target, load_sem.at[i])
        for i, (source, target) in enumerate(
            ((k_in, k_ref), (v_in, v_ref), (doc_in, doc_ref), (q_in, q_ref), (go_in, go_ref))
        )
    ]
    for load in loads:
        load.start()

    def block_rows(block):
        return pl.ds(pl.multiple_of(block * half, half), half)

    def start_of(c):
        return 2 * ((2 * count - 1 - c) // 2) - count + 2

    def block_of(d, part):
        return 2 * count - 1 - d if part else d

    def used(c, d, part):
        return c <= d if part else (d <= c) | (d >= start_of(c))

    def used_by_pair(p, d, part):
        return used(2 * p, d, part) | used(2 * p + 1, d, part)

    def ahead(step):
        return lax.rem(line + step, pairs)

    def behind(step):
        return lax.rem(line + pairs - step, pairs)

    kv[...] = jnp.zeros_like(kv)
    pair[...] = jnp.zeros_like(pair)
    recv[...] = jnp.zeros_like(recv)

    @pl.when(jnp.logical_not(has_next))
    def _():
        qg_ref[...] = jnp.zeros_like(qg_ref)
        kg_ref[...] = jnp.zeros_like(kg_ref)
        vg_ref[...] = jnp.zeros_like(vg_ref)

    barrier = pltpu.get_barrier_semaphore()
    for step in range(1, pairs):
        pl.semaphore_signal(
            barrier, inc=1, device_id={"ctx": ahead(step) * 2 + side}, device_id_type=MESH
        )
    pl.semaphore_signal(barrier, inc=1, device_id={"ctx": partner}, device_id_type=MESH)

    @pl.when(has_grads)
    def _():
        pl.semaphore_signal(barrier, inc=1, device_id={"pipe": section - 1}, device_id_type=MESH)

    @pl.when(has_next)
    def _():
        pl.semaphore_signal(barrier, inc=1, device_id={"pipe": section + 1}, device_id_type=MESH)

    loads[0].wait()
    loads[1].wait()
    for part in range(2):
        for g in range(KEY_VALUE_HEADS):
            for ref, at in ((k_ref, 0), (v_ref, 1)):
                kv[g, block_rows(block_of(me, part)), at * HEAD_SIZE:(at + 1) * HEAD_SIZE] = ref[
                    0, part * half:(part + 1) * half, g * HEAD_SIZE:(g + 1) * HEAD_SIZE
                ]

    pl.semaphore_wait(
        barrier, pairs + jnp.minimum(section, 1) + jnp.minimum(sections - 1 - section, 1)
    )

    def remote(source, target, send, receive, axis, device):
        return pltpu.make_async_remote_copy(
            src_ref=source,
            dst_ref=target,
            send_sem=send,
            recv_sem=receive,
            device_id={axis: device},
            device_id_type=MESH,
        )

    def line_copy(g, part, step, owner, target):
        block = kv.at[g, block_rows(block_of(owner, part))]
        at = (g, part, step)
        return remote(block, block, line_send.at[at], line_recv.at[at], "ctx", target)

    def side_copy(g, part, step, owner):
        block = kv.at[g, block_rows(block_of(owner, part))]
        at = (g, part, step)
        return remote(block, block, side_send.at[at], side_recv.at[at], "ctx", partner)

    def send_keys(g, act):
        for part in range(2):
            for step in range(1, pairs):
                @pl.when(used_by_pair(ahead(step), me, part))
                def _():
                    act(line_copy(g, part, step, me, ahead(step) * 2 + side))

            @pl.when(used(partner, me, part))
            def _():
                act(side_copy(g, part, 0, me))

    def pass_keys(g):
        for step in range(1, pairs):
            for part in range(2):
                owner = behind(step) * 2 + side

                @pl.when(used_by_pair(line, owner, part))
                def _():
                    line_copy(g, part, step, owner, owner).wait_recv()

                @pl.when(used(partner, owner, part))
                def _():
                    side_copy(g, part, step, owner).start()

    def wait_passed(g):
        for step in range(pairs):
            for part in range(2):
                owner = behind(step) * 2 + 1 - side

                @pl.when(used(me, owner, part))
                def _():
                    side_copy(g, part, step, owner).wait_recv()

    def wait_pass_sent(g):
        for step in range(1, pairs):
            for part in range(2):
                owner = behind(step) * 2 + side

                @pl.when(used(partner, owner, part))
                def _():
                    side_copy(g, part, step, owner).wait_send()

    for g in range(KEY_VALUE_HEADS):
        send_keys(g, lambda copy: copy.start())
    acc[...] = jnp.zeros_like(acc)
    for load in loads[2:]:
        load.wait()

    def stack(ref, part, g):
        return jnp.concatenate(
            [
                ref[0, part * half:(part + 1) * half, h * HEAD_SIZE:(h + 1) * HEAD_SIZE]
                for h in range(g * group, (g + 1) * group)
            ],
            axis=0,
        )

    def unstack(ref, part, g, value):
        for j in range(group):
            h = g * group + j
            ref[0, part * half:(part + 1) * half, h * HEAD_SIZE:(h + 1) * HEAD_SIZE] = value[
                j * half:(j + 1) * half
            ]

    def dq_copy(part, g):
        index = part * KEY_VALUE_HEADS + g
        cut = (
            slice(None),
            pl.ds(part * half, half),
            pl.ds(g * group * HEAD_SIZE, group * HEAD_SIZE),
        )
        return remote(
            dq.at[cut], qg_ref.at[cut], dq_send.at[index], dq_recv.at[index], "pipe", section - 1
        )

    def fin_copy(g, index):
        target = (kg_ref, vg_ref)[index].at[:, :, pl.ds(g * HEAD_SIZE, HEAD_SIZE)]
        return remote(
            fin.at[g, pl.ds(index, 1)], target,
            fin_send.at[g, index], fin_recv.at[g, index], "pipe", section - 1,
        )

    def unit(part, g):
        first = start_of(me) if part else 0
        own = block_of(me, part)
        base = first * half
        window = pl.ds(pl.multiple_of(base, BLK), span) if part else pl.ds(0, span)
        query = stack(q_ref, part, g)
        grad = stack(go_ref, part, g)
        keys = kv[g, window, :HEAD_SIZE]
        values = kv[g, window, HEAD_SIZE:]
        bound = jnp.int32(0)
        low = jnp.int32(0)
        for j in range(docs - 1):
            bound = bound + doc_ref[0, j] * BLK
            low = jnp.where(bound <= own * half, bound, low)
        key_pos = base + lax.broadcasted_iota(jnp.int32, (span, lanes), 0)
        query_pos = own * half + lax.broadcasted_iota(jnp.int32, (span, lanes), 1) % half
        visible = (key_pos >= low) & (key_pos <= query_pos)
        scores = dot(keys, query, ((1,), (1,))) * (scale * LOG2E)
        scores = jnp.where(visible, scores, -jnp.inf)
        top = jnp.max(scores, axis=0, keepdims=True)
        weights = jnp.exp2(scores - top)
        weights = weights * (1.0 / jnp.sum(weights, axis=0, keepdims=True))
        probs[...] = weights
        low_weights = weights.astype(BF16)
        out = dot(values.T, low_weights, ((1,), (0,))).astype(BF16)
        unstack(att_ref, part, g, out.T)

        @pl.when(has_grads)
        def _():
            delta = jnp.sum(grad.T.astype(F32) * out.astype(F32), axis=0, keepdims=True)
            weight_grad = dot(values, grad, ((1,), (1,)))
            p = probs[...]
            score_grad = (p * (weight_grad - delta) * scale).astype(BF16)
            query_grad = dot(keys.T, score_grad, ((1,), (0,))).astype(BF16)
            unstack(dq, part, g, query_grad.T)
            dq_copy(part, g).start()
            acc[g, window, :HEAD_SIZE] += dot(score_grad, query, ((1,), (0,)))
            acc[g, window, HEAD_SIZE:] += dot(p.astype(BF16), grad, ((1,), (0,)))

    def pair_copy(g, part, step, owner):
        at = (g, part, step)
        return remote(
            dkv.at[g, block_rows(block_of(owner, part))], pair.at[at],
            pair_send.at[at], pair_recv.at[at], "ctx", partner,
        )

    def sum_copy(g, part, step, owner):
        at = (g, part, step)
        return remote(
            paired.at[at], recv.at[at], sum_send.at[at], sum_recv.at[at], "ctx", owner
        )

    def terms_to_partner(g, act):
        for step in (*range(1, pairs), 0):
            for part in range(2):
                owner = ahead(step) * 2 + 1 - side

                @pl.when(used(me, owner, part))
                def _():
                    act(pair_copy(g, part, step, owner))

    def start_terms(g):
        @pl.when(has_grads)
        def _():
            dkv[g] = acc[g].astype(BF16)
            terms_to_partner(g, lambda copy: copy.start())

    def own_and_pair(g, part, step, owner):
        @pl.when(used(partner, owner, part))
        def _():
            pair_copy(g, part, step, owner).wait_recv()

        return dkv[g, block_rows(block_of(owner, part)), :].astype(F32) + pair[
            g, part, step
        ].astype(F32)

    def sums_along_line(g):
        @pl.when(has_grads)
        def _():
            for step in range(1, pairs):
                for part in range(2):
                    owner = ahead(step) * 2 + side

                    @pl.when(used_by_pair(line, owner, part))
                    def _():
                        paired[g, part, step] = own_and_pair(g, part, step, owner).astype(BF16)
                        sum_copy(g, part, step, owner).start()

    def finish(g):
        @pl.when(has_grads)
        def _():
            for part in range(2):
                total = own_and_pair(g, part, 0, me)
                for step in range(1, pairs):
                    @pl.when(used_by_pair(behind(step), me, part))
                    def _():
                        sum_copy(g, part, step, behind(step) * 2 + side).wait_recv()

                    total = total + recv[g, part, step].astype(F32)
                total = total.astype(BF16)
                fin[g, 0, part * half:(part + 1) * half, :] = total[:, :HEAD_SIZE]
                fin[g, 1, part * half:(part + 1) * half, :] = total[:, HEAD_SIZE:]
            for index in range(2):
                fin_copy(g, index).start()

    pass_keys(0)
    wait_passed(0)
    unit(1, 0)
    pass_keys(1)
    unit(0, 0)
    start_terms(0)
    wait_passed(1)
    unit(1, 1)
    sums_along_line(0)
    unit(0, 1)
    start_terms(1)
    finish(0)
    sums_along_line(1)
    finish(1)

    for g in range(KEY_VALUE_HEADS):
        send_keys(g, lambda copy: copy.wait_send())
        wait_pass_sent(g)

    @pl.when(has_grads)
    def _():
        for g in range(KEY_VALUE_HEADS):
            terms_to_partner(g, lambda copy: copy.wait_send())
            for part in range(2):
                for step in range(1, pairs):
                    owner = ahead(step) * 2 + side

                    @pl.when(used_by_pair(line, owner, part))
                    def _():
                        sum_copy(g, part, step, owner).wait_send()

                dq_copy(part, g).wait_send()
                fin_copy(g, part).wait_send()

    @pl.when(has_next)
    def _():
        for g in range(KEY_VALUE_HEADS):
            for part in range(2):
                dq_copy(part, g).wait_recv()
                fin_copy(g, part).wait_recv()


def write_out(*refs):
    size = (len(refs) - 1) // 2
    copies = [
        pltpu.make_async_copy(refs[i], refs[size + i], refs[-1].at[i]) for i in range(size)
    ]
    for copy in copies:
        copy.start()
    for copy in copies:
        copy.wait()


def solution(mesh):
    count, sections = mesh.shape["ctx"], mesh.shape["pipe"]

    def local(queries, keys, values, out_grad, doc_blocks):
        rows, columns = queries.shape[1:]
        half = rows // 2
        span = count * half
        heads = columns // HEAD_SIZE
        group = heads // KEY_VALUE_HEADS
        pairs = count // 2
        vmem = pl.BlockSpec(memory_space=pltpu.VMEM)
        hbm = pl.BlockSpec(memory_space=pltpu.HBM)
        dma = pltpu.SemaphoreType.DMA
        outputs = tuple(
            jax.ShapeDtypeStruct(x.shape, BF16) for x in (queries, queries, keys, values)
        )
        blocks = (KEY_VALUE_HEADS, 2, pairs)
        terms = (KEY_VALUE_HEADS, 2 * span, 2 * HEAD_SIZE)
        results = pl.pallas_call(
            functools.partial(kernel, count, sections, heads, doc_blocks.shape[1]),
            out_shape=outputs,
            in_specs=[hbm] * 5,
            out_specs=(vmem,) * 4,
            scratch_shapes=[
                pltpu.SMEM(doc_blocks.shape, jnp.int32),
                pltpu.VMEM(queries.shape, BF16),
                pltpu.VMEM(queries.shape, BF16),
                pltpu.VMEM(keys.shape, BF16),
                pltpu.VMEM(keys.shape, BF16),
                pltpu.VMEM(terms, BF16),
                pltpu.VMEM(terms, F32),
                pltpu.VMEM(terms, BF16),
                pltpu.VMEM((*blocks, half, 2 * HEAD_SIZE), BF16),
                pltpu.VMEM((*blocks, half, 2 * HEAD_SIZE), BF16),
                pltpu.VMEM((*blocks, half, 2 * HEAD_SIZE), BF16),
                pltpu.VMEM((span, group * half), F32),
                pltpu.VMEM(queries.shape, BF16),
                pltpu.VMEM((KEY_VALUE_HEADS, 2, rows, HEAD_SIZE), BF16),
                dma((5,)),
                *[dma(blocks)] * 8,
                *[dma((2 * KEY_VALUE_HEADS,))] * 2,
                *[dma((KEY_VALUE_HEADS, 2))] * 2,
            ],
            compiler_params=pltpu.CompilerParams(
                collective_id=0, has_side_effects=True, vmem_limit_bytes=40 << 20
            ),
        )(doc_blocks, queries, keys, values, out_grad)
        return pl.pallas_call(
            write_out,
            out_shape=outputs,
            in_specs=[vmem] * 4,
            out_specs=(hbm,) * 4,
            scratch_shapes=[dma((4,))],
        )(*results)

    split = P(("dp", "pipe"), "ctx", None)
    return jax.shard_map(
        local,
        mesh=mesh,
        in_specs=(split, split, split, split, P(("dp", "pipe"), None)),
        out_specs=(split,) * 4,
        check_vma=False,
    )
```

time: 51.9 us -> 47.6 us (0.917)
  the two profiles are of different devices: /device:TPU:28 before, /device:TPU:0 now
where the time goes in v2:
time: 47.6 us; the launch traced here: 47.2 us
  Pallas kernels  39.3 us (83%)
  local copies, waits for them, and re-layouts  7.22 us (15%)
  between operations  0.66 us (1%)
    pallas_call x1, Pallas kernels, local(): pl.pallas_call(functools.partial(kernel, count, sections, heads, doc_bloc...  37.1 us
    unnamed x18, local copies, waits for them, and re-layouts  7.22 us
    pallas_call x1, Pallas kernels, local(): pl.pallas_call(write_out, out_shape=outputs, in_specs=[vmem] * 4, out_spe...  2.23 us

profile of v2, /device:TPU:0, one launch (start us, length us, event | category | flops | bytes accessed | tf_op | source)
XLA Modules:
  0.0 47.2 jit_solution(7414652052712300187)
XLA Ops:
  0.6 0.0 copy-start
  0.6 1.0 %copy-done = bf16[1,128,2048]{2,1,0:T(8,128)(2,1)S(1)} copy-done((bf16[1,128,2048]{2,1,0:T(8,128)(2,1)S(1)}, bf16[1,128,2048]{2,1,0:T(8,128)(2,1)}, u32[]{:S(2)}) %copy-start) | copy-done | bytes 524312
  1.7 0.0 copy-start.1
  1.7 1.0 %copy-done.1 = bf16[1,128,2048]{2,1,0:T(8,128)(2,1)S(1)} copy-done((bf16[1,128,2048]{2,1,0:T(8,128)(2,1)S(1)}, bf16[1,128,2048]{2,1,0:T(8,128)(2,1)}, u32[]{:S(2)}) %copy-start.1) | copy-done | bytes 524312
  2.7 0.0 copy-start.4
  2.7 0.8 %copy-done.4 = bf16[1,128,256]{2,1,0:T(8,128)(2,1)S(1)} copy-done((bf16[1,128,256]{2,1,0:T(8,128)(2,1)S(1)}, bf16[1,128,256]{2,1,0:T(8,128)(2,1)}, u32[]{:S(2)}) %copy-start.4) | copy-done | bytes 65560
  3.6 0.0 copy-start.5
  3.6 0.8 %copy-done.5 = bf16[1,128,256]{2,1,0:T(8,128)(2,1)S(1)} copy-done((bf16[1,128,256]{2,1,0:T(8,128)(2,1)S(1)}, bf16[1,128,256]{2,1,0:T(8,128)(2,1)}, u32[]{:S(2)}) %copy-start.5) | copy-done | bytes 65560
  4.4 0.0 copy-start.8
  4.4 0.7 %copy-done.8 = s32[1,4]{1,0:T(1,128)S(1)} copy-done((s32[1,4]{1,0:T(1,128)S(1)}, s32[1,4]{1,0:T(1,128)}, u32[]{:S(2)}) %copy-start.8) | copy-done | bytes 40
  5.1 37.1 %shard_map.84 = (bf16[1,128,2048]{2,1,0:T(8,128)(2,1)S(1)}, bf16[1,128,2048]{2,1,0:T(8,128)(2,1)S(1)}, bf16[1,128,256]{2,1,0:T(8,128)(2,1)S(1)}, bf16[1,128,256]{2,1,0:T(8,128)(2,1)S(1)}) custom-call(s32[1,4]{1,0:T(1,128)S(1)} %copy-done.8, bf16[1,128,2048]{2,1,0:T(8,128)(2,1)S(1)} %copy-done, bf16[1,128,256]{2,1,0:T(8,128)(2,1)S(1)} %copy-done.4, ...), custom_call_target="tpu_custom_call" | custom-call | tf_op jit(solution)/shard_map/pallas_call | solution.py:395
  42.2 0.0 copy-start.2
  42.2 0.8 %copy-done.2 = bf16[1,128,2048]{2,1,0:T(8,128)(2,1)} copy-done((bf16[1,128,2048]{2,1,0:T(8,128)(2,1)}, bf16[1,128,2048]{2,1,0:T(8,128)(2,1)S(1)}, u32[]{:S(2)}) %copy-start.2) | copy-done | bytes 524312
  43.0 0.0 copy-start.3
  43.0 0.8 %copy-done.3 = bf16[1,128,2048]{2,1,0:T(8,128)(2,1)} copy-done((bf16[1,128,2048]{2,1,0:T(8,128)(2,1)}, bf16[1,128,2048]{2,1,0:T(8,128)(2,1)S(1)}, u32[]{:S(2)}) %copy-start.3) | copy-done | bytes 524312
  43.7 0.0 copy-start.6
  43.7 0.6 %copy-done.6 = bf16[1,128,256]{2,1,0:T(8,128)(2,1)} copy-done((bf16[1,128,256]{2,1,0:T(8,128)(2,1)}, bf16[1,128,256]{2,1,0:T(8,128)(2,1)S(1)}, u32[]{:S(2)}) %copy-start.6) | copy-done | bytes 65560
  44.4 0.0 copy-start.7
  44.4 0.6 %copy-done.7 = bf16[1,128,256]{2,1,0:T(8,128)(2,1)} copy-done((bf16[1,128,256]{2,1,0:T(8,128)(2,1)}, bf16[1,128,256]{2,1,0:T(8,128)(2,1)S(1)}, u32[]{:S(2)}) %copy-start.7) | copy-done | bytes 65560
  45.0 2.2 %shard_map.85 = (bf16[1,128,2048]{2,1,0:T(8,128)(2,1)}, bf16[1,128,2048]{2,1,0:T(8,128)(2,1)}, bf16[1,128,256]{2,1,0:T(8,128)(2,1)}, bf16[1,128,256]{2,1,0:T(8,128)(2,1)}) custom-call(bf16[1,128,2048]{2,1,0:T(8,128)(2,1)} %copy-done.2, bf16[1,128,2048]{2,1,0:T(8,128)(2,1)} %copy-done.3, bf16[1,128,256]{2,1,0:T(8,128)(2,1)} %copy-done.6, ...), custom_call_target="tpu_custom_call" | custom-call | tf_op jit(solution)/shard_map/pallas_call | solution.py:424
Async XLA Ops:
  0.6 1.0 %copy-start = (bf16[1,128,2048]{2,1,0:T(8,128)(2,1)S(1)}, bf16[1,128,2048]{2,1,0:T(8,128)(2,1)}, u32[]{:S(2)}) copy-start(bf16[1,128,2048]{2,1,0:T(8,128)(2,1)} %q_in.1) | copy-start | bytes 1572868
  1.7 1.0 %copy-start.1 = (bf16[1,128,2048]{2,1,0:T(8,128)(2,1)S(1)}, bf16[1,128,2048]{2,1,0:T(8,128)(2,1)}, u32[]{:S(2)}) copy-start(bf16[1,128,2048]{2,1,0:T(8,128)(2,1)} %go_in.1) | copy-start | bytes 1572868
  2.7 0.8 %copy-start.4 = (bf16[1,128,256]{2,1,0:T(8,128)(2,1)S(1)}, bf16[1,128,256]{2,1,0:T(8,128)(2,1)}, u32[]{:S(2)}) copy-start(bf16[1,128,256]{2,1,0:T(8,128)(2,1)} %k_in.1) | copy-start | bytes 196612
  3.6 0.8 %copy-start.5 = (bf16[1,128,256]{2,1,0:T(8,128)(2,1)S(1)}, bf16[1,128,256]{2,1,0:T(8,128)(2,1)}, u32[]{:S(2)}) copy-start(bf16[1,128,256]{2,1,0:T(8,128)(2,1)} %v_in.1) | copy-start | bytes 196612
  4.4 0.7 %copy-start.8 = (s32[1,4]{1,0:T(1,128)S(1)}, s32[1,4]{1,0:T(1,128)}, u32[]{:S(2)}) copy-start(s32[1,4]{1,0:T(1,128)} %doc_in.1) | copy-start | bytes 52
  42.2 0.8 %copy-start.2 = (bf16[1,128,2048]{2,1,0:T(8,128)(2,1)}, bf16[1,128,2048]{2,1,0:T(8,128)(2,1)S(1)}, u32[]{:S(2)}) copy-start(bf16[1,128,2048]{2,1,0:T(8,128)(2,1)S(1)} %get-tuple-element.8.refs_0_) | copy-start | bytes 1572868
  43.0 0.8 %copy-start.3 = (bf16[1,128,2048]{2,1,0:T(8,128)(2,1)}, bf16[1,128,2048]{2,1,0:T(8,128)(2,1)S(1)}, u32[]{:S(2)}) copy-start(bf16[1,128,2048]{2,1,0:T(8,128)(2,1)S(1)} %get-tuple-element.9.refs_1_) | copy-start | bytes 1572868
  43.7 0.6 %copy-start.6 = (bf16[1,128,256]{2,1,0:T(8,128)(2,1)}, bf16[1,128,256]{2,1,0:T(8,128)(2,1)S(1)}, u32[]{:S(2)}) copy-start(bf16[1,128,256]{2,1,0:T(8,128)(2,1)S(1)} %get-tuple-element.10.refs_2_) | copy-start | bytes 196612
  44.4 0.6 %copy-start.7 = (bf16[1,128,256]{2,1,0:T(8,128)(2,1)}, bf16[1,128,256]{2,1,0:T(8,128)(2,1)S(1)}, u32[]{:S(2)}) copy-start(bf16[1,128,256]{2,1,0:T(8,128)(2,1)S(1)} %get-tuple-element.11.refs_3_) | copy-start | bytes 196612

commit v3 on v2

--- a/solution.py
+++ b/solution.py
@@ -11,6 +11,7 @@
 KEY_VALUE_HEADS = 2
 HEAD_SIZE = 128
 BLK = 128
+VMEM_BYTES = 62_000_000
 LOG2E = math.log2(math.e)
 F32 = jnp.float32
 BF16 = jnp.bfloat16
@@ -23,10 +24,10 @@
 def kernel(
     count, sections, heads, docs,
     doc_in, q_in, k_in, v_in, go_in,
-    att_ref, qg_ref, kg_ref, vg_ref,
-    doc_ref, q_ref, go_ref, k_ref, v_ref,
+    att_out, qg_ref, kg_ref, vg_ref,
+    att_ref, blank, doc_ref, q_ref, go_ref, k_ref, v_ref,
     kv, acc, dkv, pair, paired, recv, probs, dq, fin,
-    load_sem, line_send, line_recv, side_send, side_recv,
+    load_sem, store_sem, line_send, line_recv, side_send, side_recv,
     pair_send, pair_recv, sum_send, sum_recv,
     dq_send, dq_recv, fin_send, fin_recv,
 ):
@@ -80,12 +81,6 @@
     pair[...] = jnp.zeros_like(pair)
     recv[...] = jnp.zeros_like(recv)
 
-    @pl.when(jnp.logical_not(has_next))
-    def _():
-        qg_ref[...] = jnp.zeros_like(qg_ref)
-        kg_ref[...] = jnp.zeros_like(kg_ref)
-        vg_ref[...] = jnp.zeros_like(vg_ref)
-
     barrier = pltpu.get_barrier_semaphore()
     for step in range(1, pairs):
         pl.semaphore_signal(
@@ -178,6 +173,25 @@
 
     for g in range(KEY_VALUE_HEADS):
         send_keys(g, lambda copy: copy.start())
+
+    columns = k_in.shape[2]
+    fills = [
+        pltpu.make_async_copy(source, target, store_sem.at[2 * KEY_VALUE_HEADS + i])
+        for i, (source, target) in enumerate(
+            (
+                (blank, qg_ref),
+                (blank.at[:, :, pl.ds(0, columns)], kg_ref),
+                (blank.at[:, :, pl.ds(0, columns)], vg_ref),
+            )
+        )
+    ]
+
+    @pl.when(jnp.logical_not(has_next))
+    def _():
+        blank[...] = jnp.zeros_like(blank)
+        for fill in fills:
+            fill.start()
+
     acc[...] = jnp.zeros_like(acc)
     for load in loads[2:]:
         load.wait()
@@ -198,13 +212,22 @@
                 j * half:(j + 1) * half
             ]
 
-    def dq_copy(part, g):
-        index = part * KEY_VALUE_HEADS + g
-        cut = (
+    def cut_of(part, g):
+        return (
             slice(None),
             pl.ds(part * half, half),
             pl.ds(g * group * HEAD_SIZE, group * HEAD_SIZE),
         )
+
+    def att_copy(part, g):
+        cut = cut_of(part, g)
+        return pltpu.make_async_copy(
+            att_ref.at[cut], att_out.at[cut], store_sem.at[part * KEY_VALUE_HEADS + g]
+        )
+
+    def dq_copy(part, g):
+        index = part * KEY_VALUE_HEADS + g
+        cut = cut_of(part, g)
         return remote(
             dq.at[cut], qg_ref.at[cut], dq_send.at[index], dq_recv.at[index], "pipe", section - 1
         )
@@ -242,6 +265,7 @@
         low_weights = weights.astype(BF16)
         out = dot(values.T, low_weights, ((1,), (0,))).astype(BF16)
         unstack(att_ref, part, g, out.T)
+        att_copy(part, g).start()
 
         @pl.when(has_grads)
         def _():
@@ -336,6 +360,15 @@
     sums_along_line(1)
     finish(1)
 
+    for part in range(2):
+        for g in range(KEY_VALUE_HEADS):
+            att_copy(part, g).wait()
+
+    @pl.when(jnp.logical_not(has_next))
+    def _():
+        for fill in fills:
+            fill.wait()
+
     for g in range(KEY_VALUE_HEADS):
         send_keys(g, lambda copy: copy.wait_send())
         wait_pass_sent(g)
@@ -384,7 +417,6 @@
         heads = columns // HEAD_SIZE
         group = heads // KEY_VALUE_HEADS
         pairs = count // 2
-        vmem = pl.BlockSpec(memory_space=pltpu.VMEM)
         hbm = pl.BlockSpec(memory_space=pltpu.HBM)
         dma = pltpu.SemaphoreType.DMA
         outputs = tuple(
@@ -396,8 +428,10 @@
             functools.partial(kernel, count, sections, heads, doc_blocks.shape[1]),
             out_shape=outputs,
             in_specs=[hbm] * 5,
-            out_specs=(vmem,) * 4,
+            out_specs=(hbm,) * 4,
             scratch_shapes=[
+                pltpu.VMEM(queries.shape, BF16),
+                pltpu.VMEM(queries.shape, BF16),
                 pltpu.SMEM(doc_blocks.shape, jnp.int32),
                 pltpu.VMEM(queries.shape, BF16),
                 pltpu.VMEM(queries.shape, BF16),
@@ -413,20 +447,22 @@
                 pltpu.VMEM(queries.shape, BF16),
                 pltpu.VMEM((KEY_VALUE_HEADS, 2, rows, HEAD_SIZE), BF16),
                 dma((5,)),
+                dma((2 * KEY_VALUE_HEADS + 3,)),
                 *[dma(blocks)] * 8,
                 *[dma((2 * KEY_VALUE_HEADS,))] * 2,
                 *[dma((KEY_VALUE_HEADS, 2))] * 2,
             ],
             compiler_params=pltpu.CompilerParams(
-                collective_id=0, has_side_effects=True, vmem_limit_bytes=40 << 20
+                collective_id=0, has_side_effects=True, vmem_limit_bytes=VMEM_BYTES
             ),
         )(doc_blocks, queries, keys, values, out_grad)
         return pl.pallas_call(
             write_out,
             out_shape=outputs,
-            in_specs=[vmem] * 4,
+            in_specs=[hbm] * 4,
             out_specs=(hbm,) * 4,
             scratch_shapes=[dma((4,))],
+            compiler_params=pltpu.CompilerParams(vmem_limit_bytes=VMEM_BYTES),
         )(*results)
 
     split = P(("dp", "pipe"), "ctx", None)

time: 47.6 us -> 74.5 us (1.57)
  Pallas kernels: 39.3 us -> 73.7 us
  local copies, waits for them, and re-layouts: 7.22 us -> 0 us
    pallas_call x1, Pallas kernels: 2.23 us -> 36.9 us  [local(): pl.pallas_call(write_out, out_shape=outputs, in_specs=[hbm] * 4, out_spec...]
    unnamed x18 -> x0, local copies, waits for them, and re-layouts: 7.22 us -> none
where the time goes in v3:
time: 74.5 us; the launch traced here: 74.4 us
  Pallas kernels  73.7 us (99%)
    pallas_call x1, Pallas kernels, local(): pl.pallas_call(write_out, out_shape=outputs, in_specs=[hbm] * 4, out_spec...  36.9 us
    pallas_call x1, Pallas kernels, local(): pl.pallas_call(functools.partial(kernel, count, sections, heads, doc_bloc...  36.8 us

profile of v3, /device:TPU:0, one launch (start us, length us, event | category | flops | bytes accessed | tf_op | source)
XLA Modules:
  0.0 74.4 jit_solution(1103578833151498418)
XLA Ops:
  0.6 36.8 %shard_map.84 = (bf16[1,128,2048]{2,1,0:T(8,128)(2,1)}, bf16[1,128,2048]{2,1,0:T(8,128)(2,1)}, bf16[1,128,256]{2,1,0:T(8,128)(2,1)}, bf16[1,128,256]{2,1,0:T(8,128)(2,1)}) custom-call(s32[1,4]{1,0:T(1,128)} %doc_in.1, bf16[1,128,2048]{2,1,0:T(8,128)(2,1)} %q_in.1, bf16[1,128,256]{2,1,0:T(8,128)(2,1)} %k_in.1, bf16[1,128,256]{2,1,0:T(8,128)(2,1)} %v_in.1, ...), custom_call_target="tpu_custom_call" | custom-call | tf_op jit(solution)/shard_map/pallas_call | solution.py:427
  37.5 36.9 %shard_map.85 = (bf16[1,128,2048]{2,1,0:T(8,128)(2,1)}, bf16[1,128,2048]{2,1,0:T(8,128)(2,1)}, bf16[1,128,256]{2,1,0:T(8,128)(2,1)}, bf16[1,128,256]{2,1,0:T(8,128)(2,1)}) custom-call(bf16[1,128,2048]{2,1,0:T(8,128)(2,1)} %get-tuple-element.8.refs_0_, bf16[1,128,2048]{2,1,0:T(8,128)(2,1)} %get-tuple-element.9.refs_1_, ...), custom_call_target="tpu_custom_call" | custom-call | tf_op jit(solution)/shard_map/pallas_call | solution.py:459

commit v4 on v3

--- a/solution.py
+++ b/solution.py
@@ -397,14 +397,22 @@
 
 
 def write_out(*refs):
-    size = (len(refs) - 1) // 2
-    copies = [
-        pltpu.make_async_copy(refs[i], refs[size + i], refs[-1].at[i]) for i in range(size)
+    size = (len(refs) - 2) // 3
+    sources, targets, held = (refs[k * size:(k + 1) * size] for k in range(3))
+    load_sem, store_sem = refs[-2:]
+    loads = [
+        pltpu.make_async_copy(sources[i], held[i], load_sem.at[i]) for i in range(size)
     ]
-    for copy in copies:
-        copy.start()
-    for copy in copies:
-        copy.wait()
+    stores = [
+        pltpu.make_async_copy(held[i], targets[i], store_sem.at[i]) for i in range(size)
+    ]
+    for load in loads:
+        load.start()
+    for load, store in zip(loads, stores):
+        load.wait()
+        store.start()
+    for store in stores:
+        store.wait()
 
 
 def solution(mesh):
@@ -461,7 +469,7 @@
             out_shape=outputs,
             in_specs=[hbm] * 4,
             out_specs=(hbm,) * 4,
-            scratch_shapes=[dma((4,))],
+            scratch_shapes=[pltpu.VMEM(x.shape, BF16) for x in outputs] + [dma((4,))] * 2,
             compiler_params=pltpu.CompilerParams(vmem_limit_bytes=VMEM_BYTES),
         )(*results)
 

time: 74.5 us -> 39.7 us (0.53)
  Pallas kernels: 73.7 us -> 38.9 us
    pallas_call x1, Pallas kernels: 36.9 us -> 2.11 us  [local(): pl.pallas_call(write_out, out_shape=outputs, in_specs=[hbm] * 4, out_spec...]
where the time goes in v4:
time: 39.7 us; the launch traced here: 39.6 us
  Pallas kernels  38.9 us (98%)
  between operations  0.64 us (2%)
    pallas_call x1, Pallas kernels, local(): pl.pallas_call(functools.partial(kernel, count, sections, heads, doc_bloc...  36.8 us
    pallas_call x1, Pallas kernels, local(): pl.pallas_call(write_out, out_shape=outputs, in_specs=[hbm] * 4, out_spec...  2.11 us

profile of v4, /device:TPU:0, one launch (start us, length us, event | category | flops | bytes accessed | tf_op | source)
XLA Modules:
  0.0 39.6 jit_solution(2841484099707418871)
XLA Ops:
  0.6 36.8 %shard_map.84 = (bf16[1,128,2048]{2,1,0:T(8,128)(2,1)}, bf16[1,128,2048]{2,1,0:T(8,128)(2,1)}, bf16[1,128,256]{2,1,0:T(8,128)(2,1)}, bf16[1,128,256]{2,1,0:T(8,128)(2,1)}) custom-call(s32[1,4]{1,0:T(1,128)} %doc_in.1, bf16[1,128,2048]{2,1,0:T(8,128)(2,1)} %q_in.1, bf16[1,128,256]{2,1,0:T(8,128)(2,1)} %k_in.1, bf16[1,128,256]{2,1,0:T(8,128)(2,1)} %v_in.1, ...), custom_call_target="tpu_custom_call" | custom-call | tf_op jit(solution)/shard_map/pallas_call | solution.py:435
  37.5 2.1 %shard_map.85 = (bf16[1,128,2048]{2,1,0:T(8,128)(2,1)}, bf16[1,128,2048]{2,1,0:T(8,128)(2,1)}, bf16[1,128,256]{2,1,0:T(8,128)(2,1)}, bf16[1,128,256]{2,1,0:T(8,128)(2,1)}) custom-call(bf16[1,128,2048]{2,1,0:T(8,128)(2,1)} %get-tuple-element.8.refs_0_, bf16[1,128,2048]{2,1,0:T(8,128)(2,1)} %get-tuple-element.9.refs_1_, ...), custom_call_target="tpu_custom_call" | custom-call | tf_op jit(solution)/shard_map/pallas_call | solution.py:467

commit v5 on v4

--- a/solution.py
+++ b/solution.py
@@ -171,8 +171,7 @@
                 def _():
                     side_copy(g, part, step, owner).wait_send()
 
-    for g in range(KEY_VALUE_HEADS):
-        send_keys(g, lambda copy: copy.start())
+    send_keys(0, lambda copy: copy.start())
 
     columns = k_in.shape[2]
     fills = [
@@ -346,6 +345,7 @@
                 fin_copy(g, index).start()
 
     pass_keys(0)
+    send_keys(1, lambda copy: copy.start())
     wait_passed(0)
     unit(1, 0)
     pass_keys(1)

time: 39.7 us -> 39.8 us (level)
  no operation moved by 1% of the time
where the time goes in v5:
time: 39.8 us; the launch traced here: 39.7 us
  Pallas kernels  39 us (98%)
  between operations  0.64 us (2%)
    pallas_call x1, Pallas kernels, local(): pl.pallas_call(functools.partial(kernel, count, sections, heads, doc_bloc...  36.9 us
    pallas_call x1, Pallas kernels, local(): pl.pallas_call(write_out, out_shape=outputs, in_specs=[hbm] * 4, out_spec...  2.11 us

profile of v5, /device:TPU:0, one launch (start us, length us, event | category | flops | bytes accessed | tf_op | source)
XLA Modules:
  0.0 39.7 jit_solution(3738801528812266100)
XLA Ops:
  0.6 36.9 %shard_map.84 = (bf16[1,128,2048]{2,1,0:T(8,128)(2,1)}, bf16[1,128,2048]{2,1,0:T(8,128)(2,1)}, bf16[1,128,256]{2,1,0:T(8,128)(2,1)}, bf16[1,128,256]{2,1,0:T(8,128)(2,1)}) custom-call(s32[1,4]{1,0:T(1,128)} %doc_in.1, bf16[1,128,2048]{2,1,0:T(8,128)(2,1)} %q_in.1, bf16[1,128,256]{2,1,0:T(8,128)(2,1)} %k_in.1, bf16[1,128,256]{2,1,0:T(8,128)(2,1)} %v_in.1, ...), custom_call_target="tpu_custom_call" | custom-call | tf_op jit(solution)/shard_map/pallas_call | solution.py:435
  37.6 2.1 %shard_map.85 = (bf16[1,128,2048]{2,1,0:T(8,128)(2,1)}, bf16[1,128,2048]{2,1,0:T(8,128)(2,1)}, bf16[1,128,256]{2,1,0:T(8,128)(2,1)}, bf16[1,128,256]{2,1,0:T(8,128)(2,1)}) custom-call(bf16[1,128,2048]{2,1,0:T(8,128)(2,1)} %get-tuple-element.8.refs_0_, bf16[1,128,2048]{2,1,0:T(8,128)(2,1)} %get-tuple-element.9.refs_1_, ...), custom_call_target="tpu_custom_call" | custom-call | tf_op jit(solution)/shard_map/pallas_call | solution.py:467
